TPU v7x, 256 devices: a whole 4x4x8 slice. The times are simulated.
256 devices in a mesh: tau: 2 (over core), row: 8 (over y, z_hi), col: 16 (over z_lo, x).
Axes of the slice: x: 4, y: 4, z: 8 (z_hi: 2, z_lo: 4; z = z_hi * 4 + z_lo), core: 2. Of those that a mesh axis runs over, the one named last changes fastest.
Arguments:
- fock: bfloat16 [12288, 12288], P('row', 'col'), as said below
- green: bfloat16 [4, 12288, 12288], P('tau', 'row', 'col'), as said below
- factors: bfloat16 [4, 12288, 768], P('tau', ('row', 'col')), may hold values from -0.21875 to 0.21875
- tile_mask: int32 [48, 48], replicated, may hold values from 0 to 1, as said below
- start_block: float32 [12288, 512], P('col'), may hold values from -1.2 to 1.2
- lower_edge: float32 [1], replicated, may hold values from -1.3 to -0.7
- upper_edge: float32 [1], replicated, may hold values from 1.7 to 2.3
Outputs:
- filtered: float32 [12288, 512], P('row')
Inputs may be any that keep to these rules, and one draw needn't show every extreme that they name: `fock`: symmetric. `green`: each of the 4 matrices is symmetric. `tile_mask`: symmetric, with every diagonal entry 1.
All inputs are finite; a program needn't handle non-finite values.
Results may differ from a plain program's by a relative error of at most 0.0072.
Values may be sent and summed in bfloat16 or wider, within the bound.
A program may use at most 128 MiB of HBM per device.

v0:
```python
import jax
import jax.numpy as jnp
from jax import lax
from jax.sharding import PartitionSpec as P

TILE = 256


def spread(value, axis, source):
    kept = jnp.where(lax.axis_index(axis) == source, value, 0).astype(value.dtype)
    return lax.psum(kept, axis)


def fold_rows(operator, rounded_rows):
    partial_value = lax.dot_general(
        operator, rounded_rows, (((0,), (0,)), ((), ())), preferred_element_type=jnp.float32
    )
    return lax.psum(partial_value, "row")


def on_device(fock, green, factors, tile_mask, start_block, lower_edge, upper_edge):
    row_id = lax.axis_index("row")
    col_id = lax.axis_index("col")
    tau_id = lax.axis_index("tau")
    n_row = lax.axis_size("row")
    n_col = lax.axis_size("col")
    n_tau = lax.axis_size("tau")
    block_rows, block_cols = fock.shape
    half_cols = block_cols // n_tau
    ratio = n_col // n_row
    row_factors = lax.all_gather(factors, "col", axis=1, tiled=True)
    piece_start = col_id % ratio * block_cols
    my_piece = lax.dynamic_slice_in_dim(row_factors, piece_start, block_cols, 1)
    col_factors = spread(my_piece, "row", col_id // ratio)
    partial_value = jnp.zeros((block_rows, block_cols), jnp.float32)
    for tau_point in range(green.shape[0]):
        product = lax.dot_general(
            row_factors[tau_point],
            col_factors[tau_point],
            (((1,), (1,)), ((), ())),
            preferred_element_type=jnp.float32,
        )
        partial_value = partial_value + product * green[tau_point].astype(jnp.float32)
    tile_rows = block_rows // TILE
    tile_cols = block_cols // TILE
    local_mask = lax.dynamic_slice(
        tile_mask, (row_id * tile_rows, col_id * tile_cols), (tile_rows, tile_cols)
    ).astype(jnp.float32)
    partial_value = (
        partial_value.reshape(tile_rows, TILE, tile_cols, TILE) * local_mask[:, None, :, None]
    ).reshape(block_rows, block_cols)
    sigma = lax.psum_scatter(partial_value, "tau", scatter_dimension=1, tiled=True)
    center = 0.5 * (upper_edge[0] + lower_edge[0])
    half_width = 0.5 * (upper_edge[0] - lower_edge[0])
    fock_half = lax.dynamic_slice_in_dim(fock, tau_id * half_cols, half_cols, 1)
    global_rows = row_id * block_rows + jnp.arange(block_rows, dtype=jnp.int32)
    global_cols = col_id * block_cols + tau_id * half_cols + jnp.arange(half_cols, dtype=jnp.int32)
    on_diagonal = global_rows[:, None] == global_cols[None, :]
    shifted = fock_half.astype(jnp.float32) + sigma - jnp.where(on_diagonal, center, 0.0)
    operator = (shifted / half_width).astype(jnp.bfloat16)
    start_rows = lax.dynamic_slice_in_dim(start_block, tau_id * half_cols, half_cols, 0)
    rounded_start = start_rows.astype(jnp.bfloat16)

    def across(rounded):
        return lax.psum(
            jnp.dot(operator, rounded, preferred_element_type=jnp.float32), ("tau", "col")
        )

    first_block = across(rounded_start)
    second_block = 2.0 * fold_rows(operator, first_block.astype(jnp.bfloat16)) - start_rows
    filtered = 2.0 * across(second_block.astype(jnp.bfloat16)) - first_block
    return filtered


def solution(mesh):
    placed = (
        P("row", "col"),
        P("tau", "row", "col"),
        P("tau", ("row", "col"), None),
        P(),
        P("col", None),
        P(),
        P(),
    )
    return jax.shard_map(
        on_device, mesh=mesh, in_specs=placed, out_specs=P("row", None), check_vma=False
    )
```

profile of v0, /device:TPU:1, one launch (start us, length us, event | category | flops | bytes accessed | tf_op | source)
XLA Modules:
  0.0 1076.6 jit_solution(9678995256825356539)
XLA Ops:
  6.5 0.0 copy-start
  6.5 0.0 all-gather.2.cloned.1.call-start
  6.5 0.7 all-gather.2.cloned.1.call-update
  7.3 0.0 all-reduce.5.cloned.1.call-start
  7.3 86.3 %all-gather.2.cloned.1.call-done = bf16[2,1536,768]{2,1,0:T(8,128)(2,1)} async-done(((bf16[2,96,768]{2,1,0:T(8,128)(2,1)}), bf16[2,1536,768]{2,1,0:T(8,128)(2,1)}) %all-gather.2.cloned.1.call-update) | async-done | bytes 4718608 | tf_op jit(solution)/shard_map/all_gather | solution.py:31
  93.6 3.5 dynamic-slice_select_fusion
  97.1 0.0 all-reduce.5.cloned.1.call-update
  97.1 0.0 reduce-scatter.2.cloned.1.call-start
  97.1 0.8 dynamic-slice_convert_fusion.2
  97.9 0.1 copy.15
  98.0 0.0 slice-start
  98.0 0.5 mul.67
  98.5 0.0 slice-start.1
  98.5 4.5 copy.19
  103.0 0.0 slice-done
  103.0 0.0 slice-done.1
  103.0 2.6 fusion.11
  105.7 4.3 copy.17
  110.0 4.3 copy.18
  114.2 202.0 %all-reduce.5.cloned.1.call-done = bf16[2,768,768]{2,1,0:T(8,128)(2,1)} async-done(((bf16[2,768,768]{2,1,0:T(8,128)(2,1)}), bf16[2,768,768]{2,1,0:T(8,128)(2,1)}) %all-reduce.5.cloned.1.call-update) | async-done | bytes 2359312 | tf_op jit(solution)/shard_map/psum | solution.py:11
  316.2 0.0 copy-start.1
  316.2 0.0 copy-start.2
  316.2 0.0 copy-start.3
  316.2 4.2 fusion.2
  320.4 0.0 copy-done.1
  320.4 0.0 copy-done.2
  320.4 0.0 copy-done.3
  320.5 7.7 fusion.1
  328.2 0.0 reduce-scatter.2.cloned.1.call-update
  328.2 0.0 all-reduce.7.cloned.1.call-start
  329.5 0.0 copy-done
  329.5 0.1 constant_dynamic-slice_fusion
  329.7 1.5 copy.16
  331.1 13.3 %reduce-scatter.2.cloned.1.call-done = f32[1536,384]{0,1:T(8,128)} async-done(((f32[1536,768]{0,1:T(8,128)}), f32[1536,384]{0,1:T(8,128)}) %reduce-scatter.2.cloned.1.call-update) | async-done | bytes 2359312 | tf_op jit(solution)/shard_map/reduce_scatter | solution.py:52
  344.4 2.5 divide_convert_fusion
  347.0 3.8 fusion.5
  350.8 0.0 all-reduce.7.cloned.1.call-update
  350.8 0.0 all-reduce.9.cloned.1.call-start
  350.8 294.9 %all-reduce.7.cloned.1.call-done = f32[1536,512]{1,0:T(8,128)} async-done(((f32[1536,512]{1,0:T(8,128)}), f32[1536,512]{1,0:T(8,128)}) %all-reduce.7.cloned.1.call-update) | async-done | bytes 3145744 | tf_op jit(solution)/shard_map/psum | solution.py:65
  645.7 3.5 fusion.3
  649.3 0.0 all-reduce.9.cloned.1.call-update
  649.3 0.0 all-reduce.11.cloned.1.call-start
  649.4 113.9 %all-reduce.9.cloned.1.call-done = f32[384,512]{1,0:T(8,128)} async-done(((f32[384,512]{1,0:T(8,128)}), f32[384,512]{1,0:T(8,128)}) %all-reduce.9.cloned.1.call-update) | async-done | bytes 786448 | tf_op jit(solution)/shard_map/psum | solution.py:18
  763.3 4.1 fusion.6
  767.3 0.0 all-reduce.11.cloned.1.call-update
  767.4 297.1 %all-reduce.11.cloned.1.call-done = f32[1536,512]{1,0:T(8,128)} async-done(((f32[1536,512]{1,0:T(8,128)}), f32[1536,512]{1,0:T(8,128)}) %all-reduce.11.cloned.1.call-update) | async-done | bytes 3145744 | tf_op jit(solution)/shard_map/psum | solution.py:65
  1064.5 5.3 multiply_subtract_fusion
  (3 shorter events, 0.0 us)
Async XLA Ops:
  6.5 323.0 %copy-start = (bf16[1536,768]{1,0:T(8,128)(2,1)S(1)}, bf16[1536,768]{1,0:T(8,128)(2,1)}, u32[]{:S(2)}) copy-start(bf16[1536,768]{1,0:T(8,128)(2,1)} %param.7) | copy-start | bytes 7077892
  6.5 87.0 %all-gather.2.cloned.1.call-start = ((), (), s32[]{:S(2)}) async-start(), calls=%async_computation.1 | async-start | bytes 5013504 | tf_op jit(solution)/shard_map/all_gather | solution.py:31
  7.3 309.0 %all-reduce.5.cloned.1.call-start = ((), (), s32[]{:S(2)}) async-start(), calls=%async_computation.2 | async-start | bytes 4718592 | tf_op jit(solution)/shard_map/psum | solution.py:11
  97.1 247.4 %reduce-scatter.2.cloned.1.call-start = ((), (), s32[]{:S(2)}) async-start(), calls=%async_computation.3 | async-start | bytes 7077888 | tf_op jit(solution)/shard_map/reduce_scatter | solution.py:52
  98.0 5.0 slice-start
  98.5 4.5 slice-start.1
  316.2 4.2 copy-start.1
  316.2 4.2 copy-start.2
  316.2 4.2 copy-start.3
  328.2 317.5 %all-reduce.7.cloned.1.call-start = ((), (), s32[]{:S(2)}) async-start(), calls=%async_computation.4 | async-start | bytes 6291456 | tf_op jit(solution)/shard_map/psum | solution.py:65
  350.8 412.5 %all-reduce.9.cloned.1.call-start = ((), (), s32[]{:S(2)}) async-start(), calls=%async_computation.5 | async-start | bytes 1572864 | tf_op jit(solution)/shard_map/psum | solution.py:18
  649.3 415.2 %all-reduce.11.cloned.1.call-start = ((), (), s32[]{:S(2)}) async-start(), calls=%async_computation.6 | async-start | bytes 6291456 | tf_op jit(solution)/shard_map/psum | solution.py:65
Sparse Core Ops, SparseCore 0:
  9.2 84.3 all-gather.1
  97.2 218.9 all-reduce.4
  328.3 16.0 reduce-scatter.1
  350.9 294.7 all-reduce.6
  649.4 113.8 all-reduce.8
  767.5 296.9 all-reduce.10
where the time goes:
time: 1080 us
  waiting for transfers between devices  1010 us (94%)
  matrix products  23.3 us (2%)
  local copies, waits for them, and re-layouts  17.9 us (2%)
  between operations  14.9 us (1%)
  other arithmetic  12 us (1%)
    psum x2, waiting for transfers between devices, across(): lax.psum(jnp.dot(operator, rounded, preferred_element_type=jnp.float32),...  592 us
    psum x1, waiting for transfers between devices, spread(): return lax.psum(kept, axis)  202 us
    psum x1, waiting for transfers between devices, fold_rows(): return lax.psum(partial_value, 'row')  114 us
    all_gather x1, waiting for transfers between devices, on_device(): row_factors = lax.all_gather(factors, 'col', axis=1, tiled=True)  86.3 us
  transfers between devices with their start and end apart: 6, of which 6 were waited for; matrix products, arithmetic and copies ran while one was open for 2% of the time, Pallas kernels for 0%

commit v1 on v0

v1 whole, which is shorter than its diff:
```python
import jax
import jax.numpy as jnp
from jax import lax
from jax.experimental import pallas as pl
from jax.experimental.pallas import tpu as pltpu
from jax.sharding import PartitionSpec as P

F32, BF16 = jnp.float32, jnp.bfloat16
NT = (((1,), (1,)), ((), ()))

PIECE = 96
SLAB = 384
BLOCK = 768
SUB = 512
TILE = 256
QUARTER = BLOCK // 4
SHARE = QUARTER // 4


def device(t, x, y, z):
    return (t, 2 * y + z // 4, 4 * (z % 4) + x)


def entry_y(x):
    return 2 * (1 - x % 2) + x // 2


def entry_x(y):
    return 2 * (y % 2) + 1 - y // 2


class Net:
    def __init__(self, send, recv):
        self.send, self.recv, self.count, self.started = send, recv, 0, []

    def put(self, src, dst, where):
        i = self.count
        self.count += 1
        copy = pltpu.make_async_remote_copy(
            src_ref=src, dst_ref=dst, send_sem=self.send.at[i], recv_sem=self.recv.at[i],
            device_id=where, device_id_type=pl.DeviceIdType.MESH,
        )
        copy.start()
        self.started.append(copy)
        return copy

    def drain(self):
        for copy in self.started:
            copy.wait_send()


class RingGather:
    def __init__(self, net, me, plus, minus, slot, source=None):
        self.net, self.me, self.plus, self.minus, self.slot = net, me, plus, minus, slot
        source = slot(me) if source is None else source
        self.up = net.put(source, slot(me), plus)
        self.down = net.put(source, slot(me), minus)

    def forward(self):
        before, after = (self.me + 3) % 4, (self.me + 1) % 4
        self.up.wait_recv()
        self.up2 = self.net.put(self.slot(before, 0), self.slot(before, 0), self.plus)
        self.down.wait_recv()
        self.down2 = self.net.put(self.slot(after, 1), self.slot(after, 1), self.minus)

    def finish(self):
        self.up2.wait_recv()
        self.down2.wait_recv()


def kernel(
    factors, green, fock, start, mask, lower, upper, out,
    frow, fcol, grn, fck, x0f, x0, sig, sgs, sgr, op, opt, part, stage, near, far, zin, zout,
    y1, y1own, part2, cstage, cin, stage2, near2, far2, hout, hin, y2, y3,
    send, recv, col_send, col_recv, local,
):
    t, r, c = lax.axis_index("tau"), lax.axis_index("row"), lax.axis_index("col")
    x, y, zl, zh = c % 4, r // 2, c // 4, r % 2
    z = 4 * zh + zl
    xp, xm = device(t, (x + 1) % 4, y, z), device(t, (x + 3) % 4, y, z)
    yp, ym = device(t, x, (y + 1) % 4, z), device(t, x, (y + 3) % 4, z)
    zls = (zl, zl + 1 - 2 * (zl % 2), (zl + 2) % 4, 3 - zl)
    zdev = [device(t, x, y, 4 * zh + s) for s in zls]
    hdev = device(t, x, y, 4 * (1 - zh) + zl)
    other = device(1 - t, x, y, z)
    targets = [device(t, z // 2, entry_y(x), y + 4 * h) for h in range(2)]
    sources = [device(t, entry_x(y), zl, 2 * x + e) for e in range(2)]

    barrier = pltpu.get_barrier_semaphore()
    greeted = [xp, xm, yp, ym, *zdev[1:], hdev, other, *targets, *sources]
    for where in greeted:
        pl.semaphore_signal(barrier, inc=1, device_id=where, device_id_type=pl.DeviceIdType.MESH)
    pl.semaphore_wait(barrier, len(greeted))

    net = Net(send, recv)

    def row_slot(slab):
        def slot(i, half=None):
            rows = pl.ds(pl.multiple_of(SLAB * slab + PIECE * i, 32), PIECE)
            return frow.at[:, rows, :] if half is None else frow.at[half, rows, :]
        return slot

    def col_slot(e):
        def slot(i, half=None):
            rows = pl.ds(pl.multiple_of(PIECE * (entry_x(i) + 4 * e), 32), PIECE)
            return fcol.at[:, rows, :] if half is None else fcol.at[half, rows, :]
        return slot

    own_col = fcol.at[:, pl.ds(pl.multiple_of(PIECE * (4 * (zl % 2) + x), 32), PIECE), :]
    col_out = [
        pltpu.make_async_remote_copy(
            src_ref=factors, dst_ref=own_col, send_sem=col_send.at[h], recv_sem=col_recv.at[zl % 2],
            device_id=targets[h], device_id_type=pl.DeviceIdType.MESH,
        )
        for h in range(2)
    ]
    for copy in col_out:
        copy.start()
    z_copies = [net.put(factors, row_slot(zl)(x), zdev[d]) for d in (1, 2, 3)]
    rings = [RingGather(net, x, xp, xm, row_slot(zl), factors)]

    own = pltpu.make_async_copy(factors, row_slot(zl)(x), local.at[0])
    own.start()
    load_green = pltpu.make_async_copy(green, grn, local.at[1])
    load_green.start()
    rows_t = pl.ds(pl.multiple_of(BLOCK * t, BLOCK), BLOCK)
    load_fock = pltpu.make_async_copy(fock.at[rows_t, :], fck, local.at[2])
    load_fock.start()
    load_start = pltpu.make_async_copy(start, x0f, local.at[3])
    load_start.start()

    z_copies[0].wait_recv()
    rings.append(RingGather(net, x, xp, xm, row_slot(zls[1])))
    cols = []
    for e in range(2):
        pltpu.make_async_remote_copy(
            src_ref=factors, dst_ref=own_col, send_sem=col_send.at[0], recv_sem=col_recv.at[e],
            device_id=targets[0], device_id_type=pl.DeviceIdType.MESH,
        ).wait_recv()
        cols.append(RingGather(net, y, yp, ym, col_slot(e)))
    rings[0].forward()
    z_copies[1].wait_recv()
    rings.append(RingGather(net, x, xp, xm, row_slot(zls[2])))
    rings[1].forward()
    z_copies[2].wait_recv()
    rings.append(RingGather(net, x, xp, xm, row_slot(zls[3])))
    for ring in cols:
        ring.forward()
    rings[2].forward()
    load_start.wait()
    x0[...] = x0f[...].astype(BF16)
    for ring in cols:
        ring.finish()

    load_green.wait()
    own.wait()

    def slab_sigma(slab):
        row0 = pl.multiple_of(SLAB * slab, 128)

        @pl.loop(0, BLOCK // TILE)
        def _(j):
            col0 = pl.multiple_of(TILE * j, TILE)
            total = jnp.zeros((SLAB, TILE), F32)
            for p in range(2):
                product = lax.dot_general(
                    frow[p, pl.ds(row0, SLAB), :], fcol[p, pl.ds(col0, TILE), :], NT, preferred_element_type=F32
                )
                total = total + product * grn[p, pl.ds(row0, SLAB), pl.ds(col0, TILE)].astype(F32)
            for b in range(SLAB // 128):
                keep = mask[6 * r + (3 * slab + b) // 2, 3 * c + j].astype(F32)
                sig[slab, pl.ds(128 * b, 128), pl.ds(col0, TILE)] = total[128 * b : 128 * (b + 1)] * keep

    def send_half():
        for u in range(2):
            sgs[u] = sig[2 * (1 - t) + u].astype(BF16)
            sig_out[u].start()

    sig_out = [
        pltpu.make_async_remote_copy(
            src_ref=sgs.at[u], dst_ref=sgr.at[u], send_sem=col_send.at[2 + u], recv_sem=col_recv.at[2 + u],
            device_id=other, device_id_type=pl.DeviceIdType.MESH,
        )
        for u in range(2)
    ]

    rings[0].finish()
    slab_sigma(zls[0])
    rings[1].finish()
    slab_sigma(zls[1])
    rings[3].forward()
    pl.when(zl // 2 != t)(send_half)
    rings[2].finish()
    slab_sigma(zls[2])
    rings[3].finish()
    slab_sigma(zls[3])
    pl.when(zl // 2 == t)(send_half)

    center = 0.5 * (upper[0] + lower[0])
    half_width = 0.5 * (upper[0] - lower[0])
    load_fock.wait()
    for u in range(2):
        sig_out[u].wait_recv()
        rows = pl.ds(SLAB * u, SLAB)
        shifted = fck[rows, :].astype(F32) + (sig[2 * t + u] + sgr[u].astype(F32))
        row_ids = lax.broadcasted_iota(jnp.int32, (SLAB, BLOCK), 0) + (2 * BLOCK * r + BLOCK * t + SLAB * u)
        col_ids = lax.broadcasted_iota(jnp.int32, (SLAB, BLOCK), 1) + BLOCK * c
        shifted = jnp.where(row_ids == col_ids, shifted - center, shifted)
        op[rows, :] = (shifted / half_width).astype(BF16)

    def ring_reduce(me, plus, minus, size, partial_rows, stage, near, far):
        h = size // 2

        def rows(i, half):
            return pl.ds(pl.multiple_of(size * i + h * half, 16), h)

        a, b, opposite = (me + 1) % 4, (me + 3) % 4, (me + 2) % 4
        stage[pl.ds(pl.multiple_of(size * opposite, 32), size), :] = partial_rows(opposite).astype(BF16)
        far_up = net.put(stage.at[rows(opposite, 0), :], far.at[0], plus)
        far_down = net.put(stage.at[rows(opposite, 1), :], far.at[1], minus)
        va = partial_rows(a)
        stage[rows(a, 1), :] = va[h:].astype(BF16)
        up1 = net.put(stage.at[rows(a, 1), :], near.at[1], plus)
        vb = partial_rows(b)
        stage[rows(b, 0), :] = vb[:h].astype(BF16)
        down0 = net.put(stage.at[rows(b, 0), :], near.at[2], minus)
        mine = partial_rows(me)
        far_up.wait_recv()
        stage[rows(a, 0), :] = (va[:h] + far[0].astype(F32)).astype(BF16)
        up0 = net.put(stage.at[rows(a, 0), :], near.at[0], plus)
        far_down.wait_recv()
        stage[rows(b, 1), :] = (vb[h:] + far[1].astype(F32)).astype(BF16)
        down1 = net.put(stage.at[rows(b, 1), :], near.at[3], minus)
        for copy in (up1, down0, up0, down1):
            copy.wait_recv()
        first = mine[:h] + near[0].astype(F32) + near[2].astype(F32)
        second = mine[h:] + near[1].astype(F32) + near[3].astype(F32)
        return first, second

    def across(block, n):
        def partial_rows(i):
            at = pl.ds(pl.multiple_of(QUARTER * i, 64), QUARTER)
            part[at, :] = jnp.dot(op[at, :], block[...], preferred_element_type=F32)
            return part[at, :]

        first, second = ring_reduce(x, xp, xm, QUARTER, partial_rows, stage.at[n], near.at[n], far.at[n])
        for i, half in enumerate((first, second)):
            part[pl.ds(2 * SHARE * i, 2 * SHARE), :] = half
            zout[n, pl.ds(2 * SHARE * i, 2 * SHARE), :] = half.astype(BF16)

        def share(s):
            return pl.ds(pl.multiple_of(SHARE * s, 16), SHARE)

        copies = [net.put(zout.at[n, share(zls[d]), :], zin.at[n, d - 1], zdev[d]) for d in (1, 2, 3)]
        total = part[share(zl), :]
        for d in (1, 2, 3):
            copies[d - 1].wait_recv()
            total = total + zin[n, d - 1].astype(F32)
        return total

    def gather_rows(buffer):
        def slots(s):
            def slot(i, half=None):
                rows = pl.ds(pl.multiple_of(QUARTER * i + SHARE * s, 16), SHARE)
                return buffer.at[rows, :] if half is None else buffer.at[rows, pl.ds(SUB // 2 * half, SUB // 2)]
            return slot

        here = slots(zl)(x)
        zc = [net.put(here, here, zdev[d]) for d in (1, 2, 3)]
        rings = [RingGather(net, x, xp, xm, slots(zl))]
        for d in (1, 2, 3):
            zc[d - 1].wait_recv()
            rings.append(RingGather(net, x, xp, xm, slots(zls[d])))
        for ring in rings:
            ring.forward()
        for ring in rings:
            ring.finish()

    my_share = pl.ds(pl.multiple_of(QUARTER * x + SHARE * zl, 16), SHARE)

    total = across(x0, 0)
    y1own[...] = total
    y1[my_share, :] = total.astype(BF16)
    for i in range(3):
        for j in range(3):
            opt[pl.ds(TILE * j, TILE), pl.ds(TILE * i, TILE)] = op[pl.ds(TILE * i, TILE), pl.ds(TILE * j, TILE)].T
    gather_rows(y1)

    far_half = pl.ds(pl.multiple_of(SLAB * (1 - t), SLAB), SLAB)
    near_half = pl.ds(pl.multiple_of(SLAB * t, SLAB), SLAB)
    cstage[...] = jnp.dot(opt[far_half, :], y1[...], preferred_element_type=F32).astype(BF16)
    swap = net.put(cstage, cin, other)
    part2[...] = jnp.dot(opt[near_half, :], y1[...], preferred_element_type=F32)
    swap.wait_recv()
    part2[...] = part2[...] + cin[...].astype(F32)
    shard = SLAB // 4

    def rows2(i):
        return part2[pl.ds(pl.multiple_of(shard * i, 32), shard), :]

    first, second = ring_reduce(y, yp, ym, shard, rows2, stage2, near2, far2)
    total = jnp.concatenate([first, second], axis=0)
    hout[...] = total.astype(BF16)
    over = net.put(hout, hin, hdev)
    over.wait_recv()
    total = total + hin[...].astype(F32)

    def slot2(i, half=None):
        rows = pl.ds(pl.multiple_of(SLAB * t + shard * i, 32), shard)
        return y2.at[rows, :] if half is None else y2.at[rows, pl.ds(SUB // 2 * half, SUB // 2)]

    mine2 = pl.ds(pl.multiple_of(SLAB * t + shard * y, 32), shard)
    y2[mine2, :] = (2.0 * total - x0f[mine2, :]).astype(BF16)
    ring = RingGather(net, y, yp, ym, slot2)
    ring.forward()
    ring.finish()
    both = net.put(y2.at[near_half, :], y2.at[near_half, :], other)
    both.wait_recv()

    total = across(y2, 1)
    here = pl.ds(pl.multiple_of(BLOCK * t + QUARTER * x + SHARE * zl, 16), SHARE)
    y3[here, :] = (2.0 * total - y1own[...]).astype(BF16)
    gather_rows(y3.at[rows_t, :])
    last = net.put(y3.at[rows_t, :], y3.at[rows_t, :], other)
    store = pltpu.make_async_copy(y3.at[rows_t, :], out.at[rows_t, :], local.at[4])
    store.start()
    last.wait_recv()
    rows_o = pl.ds(pl.multiple_of(BLOCK * (1 - t), BLOCK), BLOCK)
    store2 = pltpu.make_async_copy(y3.at[rows_o, :], out.at[rows_o, :], local.at[5])
    store2.start()
    for copy in col_out + sig_out:
        copy.wait_send()
    net.drain()
    store.wait()
    store2.wait()


def on_device(fock, green, factors, tile_mask, start_block, lower_edge, upper_edge):
    anywhere, smem = pl.BlockSpec(memory_space=pl.ANY), pl.BlockSpec(memory_space=pltpu.SMEM)
    v = pltpu.VMEM
    q2, s2 = QUARTER // 2, SLAB // 8
    result = pl.pallas_call(
        kernel,
        out_shape=jax.ShapeDtypeStruct((2 * BLOCK, SUB), BF16),
        in_specs=[anywhere] * 4 + [smem] * 3,
        out_specs=anywhere,
        scratch_shapes=[
            v((2, 2 * BLOCK, 768), BF16),
            v((2, BLOCK, 768), BF16),
            v((2, 2 * BLOCK, BLOCK), BF16),
            v((BLOCK, BLOCK), BF16),
            v((BLOCK, SUB), F32),
            v((BLOCK, SUB), BF16),
            v((4, SLAB, BLOCK), F32),
            v((2, SLAB, BLOCK), BF16),
            v((2, SLAB, BLOCK), BF16),
            v((BLOCK, BLOCK), BF16),
            v((BLOCK, BLOCK), BF16),
            v((BLOCK, SUB), F32),
            v((2, BLOCK, SUB), BF16),
            v((2, 4, q2, SUB), BF16),
            v((2, 2, q2, SUB), BF16),
            v((2, 3, SHARE, SUB), BF16),
            v((2, QUARTER, SUB), BF16),
            v((BLOCK, SUB), BF16),
            v((SHARE, SUB), F32),
            v((SLAB, SUB), F32),
            v((SLAB, SUB), BF16),
            v((SLAB, SUB), BF16),
            v((SLAB, SUB), BF16),
            v((4, s2, SUB), BF16),
            v((2, s2, SUB), BF16),
            v((2 * s2, SUB), BF16),
            v((2 * s2, SUB), BF16),
            v((BLOCK, SUB), BF16),
            v((2 * BLOCK, SUB), BF16),
            pltpu.SemaphoreType.DMA((112,)),
            pltpu.SemaphoreType.DMA((112,)),
            pltpu.SemaphoreType.DMA((4,)),
            pltpu.SemaphoreType.DMA((4,)),
            pltpu.SemaphoreType.DMA((6,)),
        ],
        compiler_params=pltpu.CompilerParams(
            collective_id=0, has_side_effects=True, vmem_limit_bytes=56 * 2**20
        ),
        name="filter_kernel",
    )(factors, green, fock, start_block, tile_mask, lower_edge, upper_edge)
    return result.astype(F32)


def solution(mesh):
    placed = (
        P("row", "col"),
        P("tau", "row", "col"),
        P("tau", ("row", "col"), None),
        P(),
        P("col", None),
        P(),
        P(),
    )
    return jax.shard_map(
        on_device, mesh=mesh, in_specs=placed, out_specs=P("row", None), check_vma=False
    )
```

time: 1080 us -> 191 us (0.18)
  waiting for transfers between devices: 1010 us -> 0 us
  Pallas kernels: 0 us -> 186 us
  matrix products: 23.3 us -> 0 us
  local copies, waits for them, and re-layouts: 17.9 us -> 0 us
  between operations: 14.9 us -> 1.3 us
    psum x4 -> x0, waiting for transfers between devices: 908 us -> none  [the longest x2 592 us: across(): lax.psum(jnp.dot(operator, rounded, preferred_element_type=jnp.float32),...]
    pallas_call x0 -> x1, Pallas kernels: none -> 186 us  [on_device(): pl.pallas_call(kernel, out_shape=jax.ShapeDtypeStruct((2 * BLOCK, SUB), B...]
    all_gather x1 -> x0, waiting for transfers between devices: 86.3 us -> none  [on_device(): row_factors = lax.all_gather(factors, 'col', axis=1, tiled=True)]
    dot_general x5 -> x0, matrix products: 23.3 us -> none  [the longest x2 11.9 us: on_device(): lax.dot_general(row_factors[tau_point], col_factors[tau_point], (((1,), (...]
    unnamed x16 -> x0, local copies, waits for them, and re-layouts: 14.6 us -> none
    reduce_scatter x1 -> x0, waiting for transfers between devices: 13.3 us -> none  [on_device(): lax.psum_scatter(partial_value, 'tau', scatter_dimension=1, tiled=True)]
  transfers between devices with their start and end apart: 6 -> 0, of which waited for: 6 -> 0; matrix products, arithmetic and copies ran while one was open for 2% -> 0% of each run, Pallas kernels for 0% -> 0%
where the time goes in v1:
time: 191 us
  Pallas kernels  186 us (97%)
  other arithmetic  3.52 us (2%)
    pallas_call x1, Pallas kernels, on_device(): pl.pallas_call(kernel, out_shape=jax.ShapeDtypeStruct((2 * BLOCK, SUB), B...  186 us

profile of v1, /device:TPU:1, one launch (start us, length us, event | category | flops | bytes accessed | tf_op | source)
XLA Modules:
  0.0 190.8 jit_solution(17563258849756588359)
XLA Ops:
  1.3 186.0 %filter_kernel.1 = bf16[1536,512]{1,0:T(8,128)(2,1)} custom-call(bf16[2,96,768]{2,1,0:T(8,128)(2,1)} %factors.1, bf16[2,1536,768]{2,1,0:T(8,128)(2,1)} %green.1, bf16[1536,768]{1,0:T(8,128)(2,1)} %fock.1, f32[768,512]{1,0:T(8,128)} %start.1, s32[48,48]{1,0:T(8,128)} %mask.1, f32[1]{0:T(128)S(6)} %copy.8.lower, f32[1]{0:T(128)S(6)} %copy.9.upper), custom_call_target="tpu_custom_call" | custom-call | tf_op jit(solution)/shard_map/filter_kernel/pallas_call | solution.py:342
  187.3 3.5 %convert_element_type.3 = f32[1536,512]{1,0:T(8,128)} convert(bf16[1536,512]{1,0:T(8,128)(2,1)} %filter_kernel.1) | non-fusion elementwise | flops 786432 | bytes 4718592 | tf_op jit(solution)/shard_map/convert_element_type | solution.py:388

commit v2 on v1

v2 whole, which is shorter than its diff:
```python
import jax
import jax.numpy as jnp
from jax import lax
from jax.experimental import pallas as pl
from jax.experimental.pallas import tpu as pltpu
from jax.sharding import PartitionSpec as P

F32, BF16 = jnp.float32, jnp.bfloat16
NT = (((1,), (1,)), ((), ()))

PIECE = 96
SLAB = 384
BLOCK = 768
SUB = 512
PARTS = 2
W = SUB // PARTS
COPIES = 28 + 70 * PARTS
TILE = 256
QUARTER = BLOCK // 4
SHARE = QUARTER // 4


def device(t, x, y, z):
    return (t, 2 * y + z // 4, 4 * (z % 4) + x)


class Net:
    def __init__(self, send, recv):
        self.send, self.recv, self.count, self.started = send, recv, 0, []

    def put(self, src, dst, where):
        i = self.count
        self.count += 1
        copy = pltpu.make_async_remote_copy(
            src_ref=src, dst_ref=dst, send_sem=self.send.at[i], recv_sem=self.recv.at[i],
            device_id=where, device_id_type=pl.DeviceIdType.MESH,
        )
        copy.start()
        self.started.append(copy)
        return copy

    def drain(self):
        assert self.count == COPIES
        for copy in self.started:
            copy.wait_send()


class RingGather:
    def __init__(self, net, me, plus, minus, slot, source=None):
        self.net, self.me, self.plus, self.minus, self.slot = net, me, plus, minus, slot
        source = slot(me) if source is None else source
        self.up = net.put(source, slot(me), plus)
        self.down = net.put(source, slot(me), minus)

    def forward(self):
        before, after = (self.me + 3) % 4, (self.me + 1) % 4
        self.up.wait_recv()
        self.up2 = self.net.put(self.slot(before, 0), self.slot(before, 0), self.plus)
        self.down.wait_recv()
        self.down2 = self.net.put(self.slot(after, 1), self.slot(after, 1), self.minus)

    def finish(self):
        self.up2.wait_recv()
        self.down2.wait_recv()


class Send:
    def __init__(self, src, dst, send_sem, recv_sem, where, is_self):
        self.is_self = is_self
        self.remote = pltpu.make_async_remote_copy(
            src_ref=src, dst_ref=dst, send_sem=send_sem, recv_sem=recv_sem,
            device_id=where, device_id_type=pl.DeviceIdType.MESH,
        )
        self.local = pltpu.make_async_copy(src, dst, recv_sem)

    def start(self):
        pl.when(self.is_self)(lambda: self.local.start())
        pl.when(jnp.logical_not(self.is_self))(lambda: self.remote.start())

    def wait_send(self):
        pl.when(jnp.logical_not(self.is_self))(lambda: self.remote.wait_send())


def in_turn(*tasks):
    tasks = list(tasks)
    while tasks:
        for task in list(tasks):
            try:
                next(task)
            except StopIteration:
                tasks.remove(task)


def kernel(
    factors, green, fock, start, mask, lower, upper, out,
    frow, fcol, fy, fz, grn, fck, x0f, x0, sig, sgs, sgr, op, opt, part, stage, near, far, zin, zout,
    y1, y1own, part2, cstage, cin, stage2, near2, far2, hout, hin, y2, y3,
    send, recv, z_send, z_recv, cy_send, cy_recv, cz_send, cz_recv, cx_send, cx_recv, sig_send, sig_recv, local,
):
    t, r, c = lax.axis_index("tau"), lax.axis_index("row"), lax.axis_index("col")
    x, y, zl, zh = c % 4, r // 2, c // 4, r % 2
    z = 4 * zh + zl
    xp, xm = device(t, (x + 1) % 4, y, z), device(t, (x + 3) % 4, y, z)
    yp, ym = device(t, x, (y + 1) % 4, z), device(t, x, (y + 3) % 4, z)
    zls = (zl, zl + 1 - 2 * (zl % 2), (zl + 2) % 4, 3 - zl)
    zdev = [device(t, x, y, 4 * zh + s) for s in zls]
    hdev = device(t, x, y, 4 * (1 - zh) + zl)
    other = device(1 - t, x, y, z)

    def by_zl(*values):
        return jnp.where(zl == 0, values[0], jnp.where(zl == 1, values[1], jnp.where(zl == 2, values[2], values[3])))

    slabs = (zl, by_zl(1, 0, 3, 2), by_zl(2, 2, 1, 1), by_zl(3, 3, 0, 0))

    entry = (x + y + z) % 4
    home_y = (y - x - z + 12) % 4
    source_z = (y - x - zl + 8) % 4
    to_x = [source_z // 2 + 2 * h for h in range(2)]

    def entry_x(at_y, e):
        return (at_y - zl - 2 * x - e + 12) % 4

    def along(i, j, k):
        return device(t, i, j, k), (i == x) & (j == y) & (k == z)

    y_to, y_from = along(x, entry, z), along(x, home_y, z)
    z_to = [along(x, y, home_y + 4 * h) for h in range(2)]
    z_from = [along(x, y, source_z + 4 * h) for h in range(2)]
    x_to = [along(to_x[h], y, z) for h in range(2)]
    x_from = [along(entry_x(y, e), y, z) for e in range(2)]

    rows_t = pl.ds(pl.multiple_of(BLOCK * t, BLOCK), BLOCK)
    load_green = pltpu.make_async_copy(green, grn, local.at[1])
    load_fock = pltpu.make_async_copy(fock.at[rows_t, :], fck, local.at[2])
    load_start = pltpu.make_async_copy(start, x0f, local.at[3])

    barrier = pltpu.get_barrier_semaphore()
    greeted = [xp, xm, yp, ym, *zdev[1:], hdev, other]
    greeted += [where for where, _ in [y_to, y_from] + z_to + z_from + x_to + x_from]
    for where in greeted:
        pl.semaphore_signal(barrier, inc=1, device_id=where, device_id_type=pl.DeviceIdType.MESH)
    pl.semaphore_wait(barrier, len(greeted))

    net = Net(send, recv)

    def row_slot(slab):
        def slot(i, half=None):
            rows = pl.ds(pl.multiple_of(SLAB * slab + PIECE * i, 32), PIECE)
            return frow.at[:, rows, :] if half is None else frow.at[half, rows, :]
        return slot

    def col_rows(e, from_x):
        return pl.ds(pl.multiple_of(PIECE * (4 * e + from_x), 32), PIECE)

    def col_slot(e):
        def slot(i, half=None):
            rows = col_rows(e, entry_x(i, e))
            return fcol.at[:, rows, :] if half is None else fcol.at[half, rows, :]
        return slot

    sends = []

    def go(src, dst, send_sem, recv_sem, target):
        copy = Send(src, dst, send_sem, recv_sem, *target)
        copy.start()
        sends.append(copy)

    def arrived(dst, recv_sem):
        pltpu.make_async_copy(dst, dst, recv_sem).wait()

    def along_z(source, slab, condition, where, i):
        copy = pltpu.make_async_remote_copy(
            src_ref=source, dst_ref=row_slot(slab)(x), send_sem=z_send.at[i], recv_sem=z_recv.at[slab],
            device_id=where, device_id_type=pl.DeviceIdType.MESH,
        )
        pl.when(condition)(lambda: copy.start())
        z_sent.append((condition, copy))

    z_sent = []
    z_up, z_down = device(t, x, y, 4 * zh + (zl + 1) % 4), device(t, x, y, 4 * zh + (zl + 3) % 4)
    along_z(factors, zl, zl < 3, z_up, 0)
    along_z(factors, zl, zl > 0, z_down, 1)
    for p in range(2):
        go(factors.at[p], fy.at[p], cy_send.at[p], cy_recv.at[p], y_to)
    rings = [RingGather(net, x, xp, xm, row_slot(zl), factors)]
    own = pltpu.make_async_copy(factors, row_slot(zl)(x), local.at[0])
    own.start()
    load_green.start()
    load_fock.start()
    load_start.start()

    def next_slab(k):
        slab = slabs[k]
        slot = row_slot(slab)(x)
        arrived(slot, z_recv.at[slab])
        up = slab < zl
        where = device(t, x, y, 4 * zh + jnp.where(up, (zl + 1) % 4, (zl + 3) % 4))
        along_z(slot, slab, jnp.where(up, zl < 3, zl > 0), where, 1 + k)
        rings.append(RingGather(net, x, xp, xm, row_slot(slab)))

    def cols_z(p):
        arrived(fy.at[p], cy_recv.at[p])
        for h in range(2):
            go(fy.at[p], fz.at[zh, p], cz_send.at[2 * h + p], cz_recv.at[2 * zh + p], z_to[h])

    def cols_x(p):
        e = source_z % 2
        for h in range(2):
            arrived(fz.at[h, p], cz_recv.at[2 * h + p])
            go(fz.at[h, p], fcol.at[p, col_rows(e, x), :], cx_send.at[2 * h + p], cx_recv.at[2 * e + p], x_to[h])

    col_up, col_down = {}, {}

    def cols_y(p):
        for e in range(2):
            mine = col_slot(e)(y, p)
            arrived(mine, cx_recv.at[2 * e + p])
            col_up[e, p] = net.put(mine, mine, yp)
            col_down[e, p] = net.put(mine, mine, ym)

    def cols_forward(p):
        copies = []
        for e in range(2):
            first, neighbour, where = (col_up[e, p], (y + 3) % 4, yp) if p == 0 else (col_down[e, p], (y + 1) % 4, ym)
            first.wait_recv()
            passed = col_slot(e)(neighbour, p)
            copies.append(net.put(passed, passed, where))
        return copies

    cols_z(0)
    next_slab(1)
    cols_z(1)
    cols_x(0)
    rings[0].forward()
    cols_x(1)
    cols_y(0)
    next_slab(2)
    rings[1].forward()
    cols_y(1)
    next_slab(3)
    far_cols = cols_forward(0) + cols_forward(1)
    rings[2].forward()
    rings[3].forward()
    load_start.wait()
    for p in range(PARTS):
        x0[p] = x0f[:, W * p : W * (p + 1)].astype(BF16)
    for e in range(2):
        col_up[e, 1].wait_recv()
        col_down[e, 0].wait_recv()
    for copy in far_cols:
        copy.wait_recv()

    load_green.wait()
    load_fock.wait()
    own.wait()

    def sig_copy(u):
        return pltpu.make_async_remote_copy(
            src_ref=sgs.at[u], dst_ref=sgr.at[u], send_sem=sig_send.at[u], recv_sem=sig_recv.at[u],
            device_id=other, device_id_type=pl.DeviceIdType.MESH,
        )

    def slab_sigma(slab):
        row0 = pl.multiple_of(SLAB * slab, 128)

        @pl.loop(0, BLOCK // TILE)
        def _(j):
            col0 = pl.multiple_of(TILE * j, TILE)
            total = jnp.zeros((SLAB, TILE), F32)
            for p in range(2):
                product = lax.dot_general(
                    frow[p, pl.ds(row0, SLAB), :], fcol[p, pl.ds(col0, TILE), :], NT, preferred_element_type=F32
                )
                total = total + product * grn[p, pl.ds(row0, SLAB), pl.ds(col0, TILE)].astype(F32)
            for b in range(SLAB // 128):
                keep = mask[6 * r + (3 * slab + b) // 2, 3 * c + j].astype(F32)
                sig[slab, pl.ds(128 * b, 128), pl.ds(col0, TILE)] = total[128 * b : 128 * (b + 1)] * keep

        @pl.when(slab // 2 != t)
        def _():
            sgs[slab % 2] = sig[slab].astype(BF16)
            sig_copy(slab % 2).start()

    center = 0.5 * (upper[0] + lower[0])
    half_width = 0.5 * (upper[0] - lower[0])

    def make_operator(which):
        for slab in which:
            u = slab % 2
            sig_copy(u).wait_recv()
            rows = pl.ds(pl.multiple_of(SLAB * u, 128), SLAB)
            shifted = fck[rows, :].astype(F32) + (sig[slab] + sgr[u].astype(F32))
            row_ids = lax.broadcasted_iota(jnp.int32, (SLAB, BLOCK), 0) + (2 * BLOCK * r + SLAB * slab)
            col_ids = lax.broadcasted_iota(jnp.int32, (SLAB, BLOCK), 1) + BLOCK * c
            shifted = jnp.where(row_ids == col_ids, shifted - center, shifted)
            op[rows, :] = (shifted / half_width).astype(BF16)

    rings[0].finish()
    slab_sigma(slabs[0])
    rings[1].finish()
    slab_sigma(slabs[1])
    pl.when(zl // 2 == t)(lambda: make_operator(slabs[:2]))
    rings[2].finish()
    slab_sigma(slabs[2])
    rings[3].finish()
    slab_sigma(slabs[3])
    pl.when(zl // 2 != t)(lambda: make_operator(slabs[2:]))

    def ring_reduce(me, plus, minus, size, ready, part, stage, near, far):
        h = size // 2

        def rows(i, half):
            return pl.ds(pl.multiple_of(size * i + h * half, 16), h)

        def push(i, half, there, where):
            return net.put(stage.at[rows(i, half), :], there, where)

        a, b, opposite = (me + 1) % 4, (me + 3) % 4, (me + 2) % 4
        ready(opposite)
        for half in range(2):
            stage[rows(opposite, half), :] = part[rows(opposite, half), :].astype(BF16)
        far_up = push(opposite, 0, far.at[0], plus)
        far_down = push(opposite, 1, far.at[1], minus)
        ready(a)
        stage[rows(a, 1), :] = part[rows(a, 1), :].astype(BF16)
        up1 = push(a, 1, near.at[1], plus)
        ready(b)
        stage[rows(b, 0), :] = part[rows(b, 0), :].astype(BF16)
        down0 = push(b, 0, near.at[2], minus)
        ready(me)
        yield
        far_up.wait_recv()
        stage[rows(a, 0), :] = (part[rows(a, 0), :] + far[0].astype(F32)).astype(BF16)
        up0 = push(a, 0, near.at[0], plus)
        far_down.wait_recv()
        stage[rows(b, 1), :] = (part[rows(b, 1), :] + far[1].astype(F32)).astype(BF16)
        down1 = push(b, 1, near.at[3], minus)
        yield
        for copy in (up1, down0, up0, down1):
            copy.wait_recv()
        for half in range(2):
            at = rows(me, half)
            part[at, :] = part[at, :] + near[half].astype(F32) + near[2 + half].astype(F32)

    def across(block, n, p):
        prt = part.at[p]

        def ready(i):
            at = pl.ds(pl.multiple_of(QUARTER * i, 64), QUARTER)
            prt[at, :] = jnp.dot(op[at, :], block[...], preferred_element_type=F32)

        k = PARTS * n + p
        yield from ring_reduce(x, xp, xm, QUARTER, ready, prt, stage.at[k], near.at[k], far.at[k])
        zout[k] = prt[pl.ds(pl.multiple_of(QUARTER * x, 64), QUARTER), :].astype(BF16)

        def share(s):
            return pl.ds(pl.multiple_of(SHARE * s, 16), SHARE)

        copies = [net.put(zout.at[k, share(zls[d]), :], zin.at[k, d - 1], zdev[d]) for d in (1, 2, 3)]
        yield
        total = prt[pl.ds(pl.multiple_of(QUARTER * x + SHARE * zl, 16), SHARE), :]
        for d in (1, 2, 3):
            copies[d - 1].wait_recv()
            total = total + zin[k, d - 1].astype(F32)
        return total

    def gather_rows(buffer):
        def slots(s):
            def slot(i, half=None):
                rows = pl.ds(pl.multiple_of(QUARTER * i + SHARE * s, 16), SHARE)
                return buffer.at[rows, :] if half is None else buffer.at[rows, pl.ds(W // 2 * half, W // 2)]
            return slot

        here = slots(zl)(x)
        zc = [net.put(here, here, zdev[d]) for d in (1, 2, 3)]
        rings = [RingGather(net, x, xp, xm, slots(zl))]
        yield
        for d in (1, 2, 3):
            zc[d - 1].wait_recv()
            rings.append(RingGather(net, x, xp, xm, slots(zls[d])))
        yield
        for ring in rings:
            ring.forward()
        yield
        for ring in rings:
            ring.finish()

    far_half = pl.ds(pl.multiple_of(SLAB * (1 - t), SLAB), SLAB)
    near_half = pl.ds(pl.multiple_of(SLAB * t, SLAB), SLAB)
    rows_o = pl.ds(pl.multiple_of(BLOCK * (1 - t), BLOCK), BLOCK)
    my_share = pl.ds(pl.multiple_of(QUARTER * x + SHARE * zl, 16), SHARE)
    my_out = pl.ds(pl.multiple_of(BLOCK * t + QUARTER * x + SHARE * zl, 16), SHARE)
    shard = SLAB // 4
    my_shard = pl.ds(pl.multiple_of(shard * y, 32), shard)
    mine2 = pl.ds(pl.multiple_of(SLAB * t + shard * y, 32), shard)
    stores = []

    def transpose():
        yield
        for i in range(3):
            for j in range(3):
                opt[pl.ds(TILE * j, TILE), pl.ds(TILE * i, TILE)] = op[pl.ds(TILE * i, TILE), pl.ds(TILE * j, TILE)].T

    def steps(p):
        cols = pl.ds(W * p, W)
        total = yield from across(x0.at[p], 0, p)
        y1own[p] = total
        y1[p, my_share, :] = total.astype(BF16)
        yield from gather_rows(y1.at[p])

        cstage[p] = jnp.dot(opt[far_half, :], y1[p], preferred_element_type=F32).astype(BF16)
        swap = net.put(cstage.at[p], cin.at[p], other)
        part2[p] = jnp.dot(opt[near_half, :], y1[p], preferred_element_type=F32)
        swap.wait_recv()
        part2[p] = part2[p] + cin[p].astype(F32)
        yield from ring_reduce(
            y, yp, ym, shard, lambda i: None, part2.at[p], stage2.at[p], near2.at[p], far2.at[p]
        )
        hout[p] = part2[p, my_shard, :].astype(BF16)
        over = net.put(hout.at[p], hin.at[p], hdev)
        yield
        over.wait_recv()
        total = part2[p, my_shard, :] + hin[p].astype(F32)

        def slot2(i, half=None):
            rows = pl.ds(pl.multiple_of(SLAB * t + shard * i, 32), shard)
            return y2.at[p, rows, :] if half is None else y2.at[p, rows, pl.ds(W // 2 * half, W // 2)]

        y2[p, mine2, :] = (2.0 * total - x0f[mine2, cols]).astype(BF16)
        ring = RingGather(net, y, yp, ym, slot2)
        yield
        ring.forward()
        yield
        ring.finish()
        both = net.put(y2.at[p, near_half, :], y2.at[p, near_half, :], other)
        yield
        both.wait_recv()

        total = yield from across(y2.at[p], 1, p)
        y3[p, my_out, :] = (2.0 * total - y1own[p]).astype(BF16)
        yield from gather_rows(y3.at[p, rows_t, :])
        last = net.put(y3.at[p, rows_t, :], y3.at[p, rows_t, :], other)
        stores.append(pltpu.make_async_copy(y3.at[p, rows_t, :], out.at[rows_t, cols], local.at[4 + 2 * p]))
        stores[-1].start()
        yield
        last.wait_recv()
        stores.append(pltpu.make_async_copy(y3.at[p, rows_o, :], out.at[rows_o, cols], local.at[5 + 2 * p]))
        stores[-1].start()

    in_turn(*[steps(p) for p in range(PARTS)], transpose())

    for copy in sends:
        copy.wait_send()
    for condition, copy in z_sent:
        pl.when(condition)(lambda: copy.wait_send())
    for u in range(2):
        sig_copy(u).wait_send()
    net.drain()
    for copy in stores:
        copy.wait()


def on_device(fock, green, factors, tile_mask, start_block, lower_edge, upper_edge):
    anywhere, smem = pl.BlockSpec(memory_space=pl.ANY), pl.BlockSpec(memory_space=pltpu.SMEM)
    v, dma = pltpu.VMEM, pltpu.SemaphoreType.DMA
    q2, s2 = QUARTER // 2, SLAB // 8
    result = pl.pallas_call(
        kernel,
        out_shape=jax.ShapeDtypeStruct((2 * BLOCK, SUB), BF16),
        in_specs=[anywhere] * 4 + [smem] * 3,
        out_specs=anywhere,
        scratch_shapes=[
            v((2, 2 * BLOCK, 768), BF16),
            v((2, BLOCK, 768), BF16),
            v((2, PIECE, 768), BF16),
            v((2, 2, PIECE, 768), BF16),
            v((2, 2 * BLOCK, BLOCK), BF16),
            v((BLOCK, BLOCK), BF16),
            v((BLOCK, SUB), F32),
            v((PARTS, BLOCK, W), BF16),
            v((4, SLAB, BLOCK), F32),
            v((2, SLAB, BLOCK), BF16),
            v((2, SLAB, BLOCK), BF16),
            v((BLOCK, BLOCK), BF16),
            v((BLOCK, BLOCK), BF16),
            v((PARTS, BLOCK, W), F32),
            v((2 * PARTS, BLOCK, W), BF16),
            v((2 * PARTS, 4, q2, W), BF16),
            v((2 * PARTS, 2, q2, W), BF16),
            v((2 * PARTS, 3, SHARE, W), BF16),
            v((2 * PARTS, QUARTER, W), BF16),
            v((PARTS, BLOCK, W), BF16),
            v((PARTS, SHARE, W), F32),
            v((PARTS, SLAB, W), F32),
            v((PARTS, SLAB, W), BF16),
            v((PARTS, SLAB, W), BF16),
            v((PARTS, SLAB, W), BF16),
            v((PARTS, 4, s2, W), BF16),
            v((PARTS, 2, s2, W), BF16),
            v((PARTS, 2 * s2, W), BF16),
            v((PARTS, 2 * s2, W), BF16),
            v((PARTS, BLOCK, W), BF16),
            v((PARTS, 2 * BLOCK, W), BF16),
            dma((COPIES,)),
            dma((COPIES,)),
            dma((5,)),
            dma((4,)),
            dma((2,)),
            dma((2,)),
            dma((4,)),
            dma((4,)),
            dma((4,)),
            dma((4,)),
            dma((2,)),
            dma((2,)),
            dma((4 + 2 * PARTS,)),
        ],
        compiler_params=pltpu.CompilerParams(
            collective_id=0, has_side_effects=True, vmem_limit_bytes=56 * 2**20
        ),
        name="filter_kernel",
    )(factors, green, fock, start_block, tile_mask, lower_edge, upper_edge)
    return result.astype(F32)


def solution(mesh):
    placed = (
        P("row", "col"),
        P("tau", "row", "col"),
        P("tau", ("row", "col"), None),
        P(),
        P("col", None),
        P(),
        P(),
    )
    return jax.shard_map(
        on_device, mesh=mesh, in_specs=placed, out_specs=P("row", None), check_vma=False
    )
```

time: 191 us -> 162 us (0.85)
  Pallas kernels: 186 us -> 157 us
    pallas_call x1, Pallas kernels: 186 us -> 157 us  [on_device(): pl.pallas_call(kernel, out_shape=jax.ShapeDtypeStruct((2 * BLOCK, SUB), B...]
where the time goes in v2:
time: 162 us; the launch traced here: 161 us
  Pallas kernels  157 us (97%)
  other arithmetic  3.52 us (2%)
    pallas_call x1, Pallas kernels, on_device(): pl.pallas_call(kernel, out_shape=jax.ShapeDtypeStruct((2 * BLOCK, SUB), B...  157 us
    convert_element_type x1, other arithmetic, on_device(): return result.astype(F32)  3.52 us

profile of v2, /device:TPU:1, one launch (start us, length us, event | category | flops | bytes accessed | tf_op | source)
XLA Modules:
  0.0 161.4 jit_solution(13770392563708539529)
XLA Ops:
  1.3 156.5 %filter_kernel.1 = bf16[1536,512]{1,0:T(8,128)(2,1)} custom-call(bf16[2,96,768]{2,1,0:T(8,128)(2,1)} %factors.1, bf16[2,1536,768]{2,1,0:T(8,128)(2,1)} %green.1, bf16[1536,768]{1,0:T(8,128)(2,1)} %fock.1, f32[768,512]{1,0:T(8,128)} %start.1, s32[48,48]{1,0:T(8,128)} %mask.1, f32[1]{0:T(128)S(6)} %copy.8.lower, f32[1]{0:T(128)S(6)} %copy.9.upper), custom_call_target="tpu_custom_call" | custom-call | tf_op jit(solution)/shard_map/filter_kernel/pallas_call | solution.py:467
  157.8 3.5 %convert_element_type.3 = f32[1536,512]{1,0:T(8,128)} convert(bf16[1536,512]{1,0:T(8,128)(2,1)} %filter_kernel.1) | non-fusion elementwise | flops 786432 | bytes 4718592 | tf_op jit(solution)/shard_map/convert_element_type | solution.py:523

commit v3 on v2

--- a/solution.py
+++ b/solution.py
@@ -9,12 +9,13 @@
 NT = (((1,), (1,)), ((), ()))
 
 PIECE = 96
+CHUNK = PIECE // 2
 SLAB = 384
 BLOCK = 768
 SUB = 512
 PARTS = 2
 W = SUB // PARTS
-COPIES = 28 + 70 * PARTS
+COPIES = 40 + 66 * PARTS
 TILE = 256
 QUARTER = BLOCK // 4
 SHARE = QUARTER // 4
@@ -62,6 +63,16 @@
     def finish(self):
         self.up2.wait_recv()
         self.down2.wait_recv()
+
+
+class DirectGather:
+    def __init__(self, net, me, plus, minus, opposite, slot):
+        mine = slot(me)
+        self.copies = [net.put(mine, mine, where) for where in (opposite, plus, minus)]
+
+    def finish(self):
+        for copy in self.copies:
+            copy.wait_recv()
 
 
 class Send:
@@ -102,6 +113,7 @@
     z = 4 * zh + zl
     xp, xm = device(t, (x + 1) % 4, y, z), device(t, (x + 3) % 4, y, z)
     yp, ym = device(t, x, (y + 1) % 4, z), device(t, x, (y + 3) % 4, z)
+    yo = device(t, x, (y + 2) % 4, z)
     zls = (zl, zl + 1 - 2 * (zl % 2), (zl + 2) % 4, 3 - zl)
     zdev = [device(t, x, y, 4 * zh + s) for s in zls]
     hdev = device(t, x, y, 4 * (1 - zh) + zl)
@@ -135,7 +147,7 @@
     load_start = pltpu.make_async_copy(start, x0f, local.at[3])
 
     barrier = pltpu.get_barrier_semaphore()
-    greeted = [xp, xm, yp, ym, *zdev[1:], hdev, other]
+    greeted = [xp, xm, yp, ym, yo, *zdev[1:], hdev, other]
     greeted += [where for where, _ in [y_to, y_from] + z_to + z_from + x_to + x_from]
     for where in greeted:
         pl.semaphore_signal(barrier, inc=1, device_id=where, device_id_type=pl.DeviceIdType.MESH)
@@ -149,14 +161,11 @@
             return frow.at[:, rows, :] if half is None else frow.at[half, rows, :]
         return slot
 
-    def col_rows(e, from_x):
-        return pl.ds(pl.multiple_of(PIECE * (4 * e + from_x), 32), PIECE)
-
-    def col_slot(e):
-        def slot(i, half=None):
-            rows = col_rows(e, entry_x(i, e))
-            return fcol.at[:, rows, :] if half is None else fcol.at[half, rows, :]
-        return slot
+    def chunk(ref, q, first=0):
+        return ref.at[q // 2, pl.ds(pl.multiple_of(first + CHUNK * (q % 2), 16), CHUNK), :]
+
+    def col_slot(e, from_x, q):
+        return chunk(fcol, q, PIECE * (4 * e + from_x))
 
     sends = []
 
@@ -180,8 +189,8 @@
     z_up, z_down = device(t, x, y, 4 * zh + (zl + 1) % 4), device(t, x, y, 4 * zh + (zl + 3) % 4)
     along_z(factors, zl, zl < 3, z_up, 0)
     along_z(factors, zl, zl > 0, z_down, 1)
-    for p in range(2):
-        go(factors.at[p], fy.at[p], cy_send.at[p], cy_recv.at[p], y_to)
+    for q in range(4):
+        go(chunk(factors, q), chunk(fy, q), cy_send.at[q], cy_recv.at[q], y_to)
     rings = [RingGather(net, x, xp, xm, row_slot(zl), factors)]
     own = pltpu.make_async_copy(factors, row_slot(zl)(x), local.at[0])
     own.start()
@@ -198,55 +207,60 @@
         along_z(slot, slab, jnp.where(up, zl < 3, zl > 0), where, 1 + k)
         rings.append(RingGather(net, x, xp, xm, row_slot(slab)))
 
-    def cols_z(p):
-        arrived(fy.at[p], cy_recv.at[p])
+    def cols_z(q):
+        arrived(chunk(fy, q), cy_recv.at[q])
         for h in range(2):
-            go(fy.at[p], fz.at[zh, p], cz_send.at[2 * h + p], cz_recv.at[2 * zh + p], z_to[h])
-
-    def cols_x(p):
+            go(chunk(fy, q), chunk(fz.at[zh], q), cz_send.at[4 * h + q], cz_recv.at[4 * zh + q], z_to[h])
+
+    def cols_x(q):
         e = source_z % 2
         for h in range(2):
-            arrived(fz.at[h, p], cz_recv.at[2 * h + p])
-            go(fz.at[h, p], fcol.at[p, col_rows(e, x), :], cx_send.at[2 * h + p], cx_recv.at[2 * e + p], x_to[h])
-
-    col_up, col_down = {}, {}
-
-    def cols_y(p):
+            arrived(chunk(fz.at[h], q), cz_recv.at[4 * h + q])
+            go(chunk(fz.at[h], q), col_slot(e, x, q), cx_send.at[4 * h + q], cx_recv.at[4 * e + q], x_to[h])
+
+    col_up, col_down, far_cols = {}, {}, []
+
+    def cols_y(q):
         for e in range(2):
-            mine = col_slot(e)(y, p)
-            arrived(mine, cx_recv.at[2 * e + p])
-            col_up[e, p] = net.put(mine, mine, yp)
-            col_down[e, p] = net.put(mine, mine, ym)
-
-    def cols_forward(p):
-        copies = []
+            mine = col_slot(e, entry_x(y, e), q)
+            arrived(mine, cx_recv.at[4 * e + q])
+            col_up[e, q] = net.put(mine, mine, yp)
+            col_down[e, q] = net.put(mine, mine, ym)
+
+    def cols_forward(q):
         for e in range(2):
-            first, neighbour, where = (col_up[e, p], (y + 3) % 4, yp) if p == 0 else (col_down[e, p], (y + 1) % 4, ym)
+            first, neighbour, where = (col_down[e, q], (y + 1) % 4, ym) if q % 2 else (col_up[e, q], (y + 3) % 4, yp)
             first.wait_recv()
-            passed = col_slot(e)(neighbour, p)
-            copies.append(net.put(passed, passed, where))
-        return copies
-
-    cols_z(0)
+            passed = col_slot(e, entry_x(neighbour, e), q)
+            far_cols.append(net.put(passed, passed, where))
+
+    for q in range(4):
+        cols_z(q)
+    rings[0].forward()
     next_slab(1)
-    cols_z(1)
     cols_x(0)
-    rings[0].forward()
     cols_x(1)
     cols_y(0)
+    cols_x(2)
+    cols_y(1)
+    cols_x(3)
+    rings[1].forward()
     next_slab(2)
-    rings[1].forward()
-    cols_y(1)
+    cols_y(2)
+    cols_forward(0)
+    cols_y(3)
+    cols_forward(1)
     next_slab(3)
-    far_cols = cols_forward(0) + cols_forward(1)
     rings[2].forward()
+    cols_forward(2)
+    cols_forward(3)
     rings[3].forward()
     load_start.wait()
     for p in range(PARTS):
         x0[p] = x0f[:, W * p : W * (p + 1)].astype(BF16)
     for e in range(2):
-        col_up[e, 1].wait_recv()
-        col_down[e, 0].wait_recv()
+        for q in range(4):
+            (col_up if q % 2 else col_down)[e, q].wait_recv()
     for copy in far_cols:
         copy.wait_recv()
 
@@ -305,6 +319,23 @@
     rings[3].finish()
     slab_sigma(slabs[3])
     pl.when(zl // 2 != t)(lambda: make_operator(slabs[2:]))
+
+    def direct_reduce(me, plus, minus, opposite, size, ready, part, stage, near, far):
+        def rows(i):
+            return pl.ds(pl.multiple_of(size * i, 32), size)
+
+        copies = []
+        for k, where, into in ((2, opposite, far), (1, plus, near.at[0]), (3, minus, near.at[1])):
+            at = rows((me + k) % 4)
+            ready((me + k) % 4)
+            stage[at, :] = part[at, :].astype(BF16)
+            copies.append(net.put(stage.at[at, :], into, where))
+        ready(me)
+        yield
+        for copy in copies:
+            copy.wait_recv()
+        at = rows(me)
+        part[at, :] = part[at, :] + far[...].astype(F32) + (near[0].astype(F32) + near[1].astype(F32))
 
     def ring_reduce(me, plus, minus, size, ready, part, stage, near, far):
         h = size // 2
@@ -413,8 +444,8 @@
         part2[p] = jnp.dot(opt[near_half, :], y1[p], preferred_element_type=F32)
         swap.wait_recv()
         part2[p] = part2[p] + cin[p].astype(F32)
-        yield from ring_reduce(
-            y, yp, ym, shard, lambda i: None, part2.at[p], stage2.at[p], near2.at[p], far2.at[p]
+        yield from direct_reduce(
+            y, yp, ym, yo, shard, lambda i: None, part2.at[p], stage2.at[p], near2.at[p], far2.at[p]
         )
         hout[p] = part2[p, my_shard, :].astype(BF16)
         over = net.put(hout.at[p], hin.at[p], hdev)
@@ -427,9 +458,7 @@
             return y2.at[p, rows, :] if half is None else y2.at[p, rows, pl.ds(W // 2 * half, W // 2)]
 
         y2[p, mine2, :] = (2.0 * total - x0f[mine2, cols]).astype(BF16)
-        ring = RingGather(net, y, yp, ym, slot2)
-        yield
-        ring.forward()
+        ring = DirectGather(net, y, yp, ym, yo, slot2)
         yield
         ring.finish()
         both = net.put(y2.at[p, near_half, :], y2.at[p, near_half, :], other)
@@ -495,8 +524,8 @@
             v((PARTS, SLAB, W), BF16),
             v((PARTS, SLAB, W), BF16),
             v((PARTS, SLAB, W), BF16),
-            v((PARTS, 4, s2, W), BF16),
-            v((PARTS, 2, s2, W), BF16),
+            v((PARTS, 2, 2 * s2, W), BF16),
+            v((PARTS, 2 * s2, W), BF16),
             v((PARTS, 2 * s2, W), BF16),
             v((PARTS, 2 * s2, W), BF16),
             v((PARTS, BLOCK, W), BF16),
@@ -505,18 +534,18 @@
             dma((COPIES,)),
             dma((5,)),
             dma((4,)),
-            dma((2,)),
-            dma((2,)),
             dma((4,)),
             dma((4,)),
-            dma((4,)),
-            dma((4,)),
+            dma((8,)),
+            dma((8,)),
+            dma((8,)),
+            dma((8,)),
             dma((2,)),
             dma((2,)),
             dma((4 + 2 * PARTS,)),
         ],
         compiler_params=pltpu.CompilerParams(
-            collective_id=0, has_side_effects=True, vmem_limit_bytes=56 * 2**20
+            collective_id=0, has_side_effects=True, vmem_limit_bytes=52 * 2**20
         ),
         name="filter_kernel",
     )(factors, green, fock, start_block, tile_mask, lower_edge, upper_edge)

time: 162 us -> 155 us (0.957)
  Pallas kernels: 157 us -> 150 us
  local copies, waits for them, and re-layouts: 0 us -> 1.69 us
    pallas_call x1, Pallas kernels: 157 us -> 150 us  [on_device(): pl.pallas_call(kernel, out_shape=jax.ShapeDtypeStruct((2 * BLOCK, SUB), B...]
    unnamed x0 -> x4, local copies, waits for them, and re-layouts: none -> 1.69 us
where the time goes in v3:
time: 155 us
  Pallas kernels  150 us (97%)
  other arithmetic  2.11 us (1%)
  local copies, waits for them, and re-layouts  1.69 us (1%)
    pallas_call x1, Pallas kernels, on_device(): pl.pallas_call(kernel, out_shape=jax.ShapeDtypeStruct((2 * BLOCK, SUB), B...  150 us

profile of v3, /device:TPU:1, one launch (start us, length us, event | category | flops | bytes accessed | tf_op | source)
XLA Modules:
  0.0 154.9 jit_solution(4367818842793139478)
XLA Ops:
  1.3 0.0 copy-start
  1.3 1.0 copy-done
  2.3 0.0 copy-start.1
  2.3 0.7 copy-done.1
  3.0 149.8 %filter_kernel.1 = bf16[1536,512]{1,0:T(8,128)(2,1)S(1)} custom-call(bf16[2,96,768]{2,1,0:T(8,128)(2,1)S(1)} %copy-done, bf16[2,1536,768]{2,1,0:T(8,128)(2,1)} %green.1, bf16[1536,768]{1,0:T(8,128)(2,1)} %fock.1, f32[768,512]{1,0:T(8,128)} %start.1, s32[48,48]{1,0:T(8,128)S(1)} %copy-done.1, f32[1]{0:T(128)S(6)} %copy.8.lower, f32[1]{0:T(128)S(6)} %copy.9.upper), custom_call_target="tpu_custom_call" | custom-call | tf_op jit(solution)/shard_map/filter_kernel/pallas_call | solution.py:496
  152.8 2.1 %convert_element_type.3 = f32[1536,512]{1,0:T(8,128)} convert(bf16[1536,512]{1,0:T(8,128)(2,1)S(1)} %filter_kernel.1) | non-fusion elementwise | flops 786432 | bytes 4718592 | tf_op jit(solution)/shard_map/convert_element_type | solution.py:552
Async XLA Ops:
  1.3 1.0 copy-start
  2.3 0.7 copy-start.1

commit v4 on v3

--- a/solution.py
+++ b/solution.py
@@ -15,7 +15,7 @@
 SUB = 512
 PARTS = 2
 W = SUB // PARTS
-COPIES = 40 + 66 * PARTS
+COPIES = 48 + 66 * PARTS
 TILE = 256
 QUARTER = BLOCK // 4
 SHARE = QUARTER // 4
@@ -63,6 +63,23 @@
     def finish(self):
         self.up2.wait_recv()
         self.down2.wait_recv()
+
+
+class SplitRingGather(RingGather):
+    def __init__(self, net, me, plus, minus, slot, source=None):
+        self.net, self.me, self.plus, self.minus, self.slot = net, me, plus, minus, slot
+
+        def half(h, where):
+            src = slot(me, h) if source is None else source.at[h]
+            return net.put(src, slot(me, h), where)
+
+        self.up, self.down = half(0, plus), half(1, minus)
+        self.rest = [half(1, plus), half(0, minus)]
+
+    def finish(self):
+        for copy in self.rest:
+            copy.wait_recv()
+        super().finish()
 
 
 class DirectGather:
@@ -191,7 +208,7 @@
     along_z(factors, zl, zl > 0, z_down, 1)
     for q in range(4):
         go(chunk(factors, q), chunk(fy, q), cy_send.at[q], cy_recv.at[q], y_to)
-    rings = [RingGather(net, x, xp, xm, row_slot(zl), factors)]
+    rings = [SplitRingGather(net, x, xp, xm, row_slot(zl), factors)]
     own = pltpu.make_async_copy(factors, row_slot(zl)(x), local.at[0])
     own.start()
     load_green.start()
@@ -205,7 +222,7 @@
         up = slab < zl
         where = device(t, x, y, 4 * zh + jnp.where(up, (zl + 1) % 4, (zl + 3) % 4))
         along_z(slot, slab, jnp.where(up, zl < 3, zl > 0), where, 1 + k)
-        rings.append(RingGather(net, x, xp, xm, row_slot(slab)))
+        rings.append(SplitRingGather(net, x, xp, xm, row_slot(slab)))
 
     def cols_z(q):
         arrived(chunk(fy, q), cy_recv.at[q])
@@ -286,13 +303,22 @@
                     frow[p, pl.ds(row0, SLAB), :], fcol[p, pl.ds(col0, TILE), :], NT, preferred_element_type=F32
                 )
                 total = total + product * grn[p, pl.ds(row0, SLAB), pl.ds(col0, TILE)].astype(F32)
+            bands = []
             for b in range(SLAB // 128):
                 keep = mask[6 * r + (3 * slab + b) // 2, 3 * c + j].astype(F32)
-                sig[slab, pl.ds(128 * b, 128), pl.ds(col0, TILE)] = total[128 * b : 128 * (b + 1)] * keep
+                bands.append(total[128 * b : 128 * (b + 1)] * keep)
+            kept = jnp.concatenate(bands, axis=0)
+
+            @pl.when(slab // 2 == t)
+            def _():
+                sig[slab % 2, :, pl.ds(col0, TILE)] = kept
+
+            @pl.when(slab // 2 != t)
+            def _():
+                sgs[slab % 2, :, pl.ds(col0, TILE)] = kept.astype(BF16)
 
         @pl.when(slab // 2 != t)
         def _():
-            sgs[slab % 2] = sig[slab].astype(BF16)
             sig_copy(slab % 2).start()
 
     center = 0.5 * (upper[0] + lower[0])
@@ -303,7 +329,7 @@
             u = slab % 2
             sig_copy(u).wait_recv()
             rows = pl.ds(pl.multiple_of(SLAB * u, 128), SLAB)
-            shifted = fck[rows, :].astype(F32) + (sig[slab] + sgr[u].astype(F32))
+            shifted = fck[rows, :].astype(F32) + (sig[u] + sgr[u].astype(F32))
             row_ids = lax.broadcasted_iota(jnp.int32, (SLAB, BLOCK), 0) + (2 * BLOCK * r + SLAB * slab)
             col_ids = lax.broadcasted_iota(jnp.int32, (SLAB, BLOCK), 1) + BLOCK * c
             shifted = jnp.where(row_ids == col_ids, shifted - center, shifted)
@@ -507,7 +533,7 @@
             v((BLOCK, BLOCK), BF16),
             v((BLOCK, SUB), F32),
             v((PARTS, BLOCK, W), BF16),
-            v((4, SLAB, BLOCK), F32),
+            v((2, SLAB, BLOCK), F32),
             v((2, SLAB, BLOCK), BF16),
             v((2, SLAB, BLOCK), BF16),
             v((BLOCK, BLOCK), BF16),

time: 155 us -> 153 us (0.987)
  Pallas kernels: 150 us -> 148 us
    pallas_call x1, Pallas kernels: 150 us -> 148 us  [on_device(): pl.pallas_call(kernel, out_shape=jax.ShapeDtypeStruct((2 * BLOCK, SUB), B...]
where the time goes in v4:
time: 153 us
  Pallas kernels  148 us (97%)
  other arithmetic  2.11 us (1%)
  local copies, waits for them, and re-layouts  1.69 us (1%)
    pallas_call x1, Pallas kernels, on_device(): pl.pallas_call(kernel, out_shape=jax.ShapeDtypeStruct((2 * BLOCK, SUB), B...  148 us

profile of v4, /device:TPU:1, one launch (start us, length us, event | category | flops | bytes accessed | tf_op | source)
XLA Modules:
  0.0 152.8 jit_solution(9044421884916089947)
XLA Ops:
  1.3 0.0 copy-start
  1.3 1.0 copy-done
  2.3 0.0 copy-start.1
  2.3 0.7 copy-done.1
  3.0 147.6 %filter_kernel.1 = bf16[1536,512]{1,0:T(8,128)(2,1)S(1)} custom-call(bf16[2,96,768]{2,1,0:T(8,128)(2,1)S(1)} %copy-done, bf16[2,1536,768]{2,1,0:T(8,128)(2,1)} %green.1, bf16[1536,768]{1,0:T(8,128)(2,1)} %fock.1, f32[768,512]{1,0:T(8,128)} %start.1, s32[48,48]{1,0:T(8,128)S(1)} %copy-done.1, f32[1]{0:T(128)S(6)} %copy.8.lower, f32[1]{0:T(128)S(6)} %copy.9.upper), custom_call_target="tpu_custom_call" | custom-call | tf_op jit(solution)/shard_map/filter_kernel/pallas_call | solution.py:522
  150.6 2.1 %convert_element_type.3 = f32[1536,512]{1,0:T(8,128)} convert(bf16[1536,512]{1,0:T(8,128)(2,1)S(1)} %filter_kernel.1) | non-fusion elementwise | flops 786432 | bytes 4718592 | tf_op jit(solution)/shard_map/convert_element_type | solution.py:578
Async XLA Ops:
  1.3 1.0 copy-start
  2.3 0.7 copy-start.1

commit v5 on v4

--- a/solution.py
+++ b/solution.py
@@ -15,7 +15,7 @@
 SUB = 512
 PARTS = 2
 W = SUB // PARTS
-COPIES = 48 + 66 * PARTS
+COPIES = 48 + 72 * PARTS
 TILE = 256
 QUARTER = BLOCK // 4
 SHARE = QUARTER // 4
@@ -86,10 +86,6 @@
     def __init__(self, net, me, plus, minus, opposite, slot):
         mine = slot(me)
         self.copies = [net.put(mine, mine, where) for where in (opposite, plus, minus)]
-
-    def finish(self):
-        for copy in self.copies:
-            copy.wait_recv()
 
 
 class Send:
@@ -421,7 +417,7 @@
             total = total + zin[k, d - 1].astype(F32)
         return total
 
-    def gather_rows(buffer):
+    def gather_rows(buffer, complete=lambda i: None):
         def slots(s):
             def slot(i, half=None):
                 rows = pl.ds(pl.multiple_of(QUARTER * i + SHARE * s, 16), SHARE)
@@ -435,12 +431,16 @@
         for d in (1, 2, 3):
             zc[d - 1].wait_recv()
             rings.append(RingGather(net, x, xp, xm, slots(zls[d])))
+        complete(x)
         yield
         for ring in rings:
             ring.forward()
+        complete((x + 3) % 4)
+        complete((x + 1) % 4)
         yield
         for ring in rings:
             ring.finish()
+        complete((x + 2) % 4)
 
     far_half = pl.ds(pl.multiple_of(SLAB * (1 - t), SLAB), SLAB)
     near_half = pl.ds(pl.multiple_of(SLAB * t, SLAB), SLAB)
@@ -486,19 +486,28 @@
         y2[p, mine2, :] = (2.0 * total - x0f[mine2, cols]).astype(BF16)
         ring = DirectGather(net, y, yp, ym, yo, slot2)
         yield
-        ring.finish()
-        both = net.put(y2.at[p, near_half, :], y2.at[p, near_half, :], other)
-        yield
-        both.wait_recv()
+        both = [net.put(slot2(y), slot2(y), other)]
+        for copy, i in zip(ring.copies[1:] + ring.copies[:1], (y + 3, y + 1, y + 2)):
+            copy.wait_recv()
+            both.append(net.put(slot2(i % 4), slot2(i % 4), other))
+        yield
+        for copy in both:
+            copy.wait_recv()
 
         total = yield from across(y2.at[p], 1, p)
         y3[p, my_out, :] = (2.0 * total - y1own[p]).astype(BF16)
-        yield from gather_rows(y3.at[p, rows_t, :])
-        last = net.put(y3.at[p, rows_t, :], y3.at[p, rows_t, :], other)
+        last = []
+
+        def pass_on(i):
+            quarter = y3.at[p, pl.ds(pl.multiple_of(BLOCK * t + QUARTER * i, 64), QUARTER), :]
+            last.append(net.put(quarter, quarter, other))
+
+        yield from gather_rows(y3.at[p, rows_t, :], pass_on)
         stores.append(pltpu.make_async_copy(y3.at[p, rows_t, :], out.at[rows_t, cols], local.at[4 + 2 * p]))
         stores[-1].start()
         yield
-        last.wait_recv()
+        for copy in last:
+            copy.wait_recv()
         stores.append(pltpu.make_async_copy(y3.at[p, rows_o, :], out.at[rows_o, cols], local.at[5 + 2 * p]))
         stores[-1].start()
 

time: 153 us -> 152 us (level)
  no operation moved by 1% of the time
where the time goes in v5:
time: 152 us
  Pallas kernels  147 us (97%)
  other arithmetic  2.11 us (1%)
  local copies, waits for them, and re-layouts  1.69 us (1%)
    pallas_call x1, Pallas kernels, on_device(): pl.pallas_call(kernel, out_shape=jax.ShapeDtypeStruct((2 * BLOCK, SUB), B...  147 us

profile of v5, /device:TPU:1, one launch (start us, length us, event | category | flops | bytes accessed | tf_op | source)
XLA Modules:
  0.0 152.0 jit_solution(3540717083169500017)
XLA Ops:
  1.3 0.0 copy-start
  1.3 1.0 copy-done
  2.3 0.0 copy-start.1
  2.3 0.7 copy-done.1
  3.0 146.9 %filter_kernel.1 = bf16[1536,512]{1,0:T(8,128)(2,1)S(1)} custom-call(bf16[2,96,768]{2,1,0:T(8,128)(2,1)S(1)} %copy-done, bf16[2,1536,768]{2,1,0:T(8,128)(2,1)} %green.1, bf16[1536,768]{1,0:T(8,128)(2,1)} %fock.1, f32[768,512]{1,0:T(8,128)} %start.1, s32[48,48]{1,0:T(8,128)S(1)} %copy-done.1, f32[1]{0:T(128)S(6)} %copy.8.lower, f32[1]{0:T(128)S(6)} %copy.9.upper), custom_call_target="tpu_custom_call" | custom-call | tf_op jit(solution)/shard_map/filter_kernel/pallas_call | solution.py:531
  149.9 2.1 %convert_element_type.3 = f32[1536,512]{1,0:T(8,128)} convert(bf16[1536,512]{1,0:T(8,128)(2,1)S(1)} %filter_kernel.1) | non-fusion elementwise | flops 786432 | bytes 4718592 | tf_op jit(solution)/shard_map/convert_element_type | solution.py:587
Async XLA Ops:
  1.3 1.0 copy-start
  2.3 0.7 copy-start.1

commit v6 on v5

--- a/solution.py
+++ b/solution.py
@@ -468,6 +468,7 @@
         cstage[p] = jnp.dot(opt[far_half, :], y1[p], preferred_element_type=F32).astype(BF16)
         swap = net.put(cstage.at[p], cin.at[p], other)
         part2[p] = jnp.dot(opt[near_half, :], y1[p], preferred_element_type=F32)
+        yield
         swap.wait_recv()
         part2[p] = part2[p] + cin[p].astype(F32)
         yield from direct_reduce(

time: 152 us -> 153 us (level)
  no operation moved by 1% of the time
where the time goes in v6:
time: 153 us
  Pallas kernels  148 us (97%)
  other arithmetic  2.11 us (1%)
  local copies, waits for them, and re-layouts  1.69 us (1%)
    pallas_call x1, Pallas kernels, on_device(): pl.pallas_call(kernel, out_shape=jax.ShapeDtypeStruct((2 * BLOCK, SUB), B...  148 us

profile of v6, /device:TPU:1, one launch (start us, length us, event | category | flops | bytes accessed | tf_op | source)
XLA Modules:
  0.0 152.6 jit_solution(17263553000224957729)
XLA Ops:
  1.3 0.0 copy-start
  1.3 1.0 copy-done
  2.3 0.0 copy-start.1
  2.3 0.7 copy-done.1
  3.0 147.5 %filter_kernel.1 = bf16[1536,512]{1,0:T(8,128)(2,1)S(1)} custom-call(bf16[2,96,768]{2,1,0:T(8,128)(2,1)S(1)} %copy-done, bf16[2,1536,768]{2,1,0:T(8,128)(2,1)} %green.1, bf16[1536,768]{1,0:T(8,128)(2,1)} %fock.1, f32[768,512]{1,0:T(8,128)} %start.1, s32[48,48]{1,0:T(8,128)S(1)} %copy-done.1, f32[1]{0:T(128)S(6)} %copy.8.lower, f32[1]{0:T(128)S(6)} %copy.9.upper), custom_call_target="tpu_custom_call" | custom-call | tf_op jit(solution)/shard_map/filter_kernel/pallas_call | solution.py:532
  150.5 2.1 %convert_element_type.3 = f32[1536,512]{1,0:T(8,128)} convert(bf16[1536,512]{1,0:T(8,128)(2,1)S(1)} %filter_kernel.1) | non-fusion elementwise | flops 786432 | bytes 4718592 | tf_op jit(solution)/shard_map/convert_element_type | solution.py:588
Async XLA Ops:
  1.3 1.0 copy-start
  2.3 0.7 copy-start.1
